TPU v7x, 32 devices: a whole 2x2x4 slice. The times are simulated.
32 devices in a mesh: dp: 8 (over y, x, core), chan: 4 (over z).
Axes of the slice: x: 2, y: 2, z: 4, core: 2. Of those that a mesh axis runs over, the one named last changes fastest.
Arguments:
- features: bfloat16 [25088, 512], P('dp', 'chan'), may hold values from -6 to 6
- cotangent: float32 [25088, 512], P('dp', 'chan'), may hold values from -6 to 6
- clip_frames: int32 [128], P('dp'), may hold values from 8 to 32, as said below
- spatial_master: float32 [2, 4608, 1152], P(None, 'dp', 'chan'), may hold values from -0.09375 to 0.09375
- spatial_first: float32 [2, 4608, 1152], P(None, 'dp', 'chan'), may hold values from -32 to 32
- spatial_second: float32 [2, 4608, 1152], P(None, 'dp', 'chan'), may hold values from 125.44 to 501.76
- temporal_master: float32 [2, 3, 1152, 512], P(None, None, 'chan', 'dp'), may hold values from -0.109375 to 0.109375
- temporal_first: float32 [2, 3, 1152, 512], P(None, None, 'chan', 'dp'), may hold values from -32 to 32
- temporal_second: float32 [2, 3, 1152, 512], P(None, None, 'chan', 'dp'), may hold values from 125.44 to 501.76
- mid_norm: float32 [4, 1152], P(None, 'chan'), may hold values from 0.5 to 1.5
- mid_first: float32 [4, 1152], P(None, 'chan'), may hold values from -32 to 32
- mid_second: float32 [4, 1152], P(None, 'chan'), may hold values from 125.44 to 501.76
- out_norm: float32 [4, 512], P(None, 'chan'), may hold values from 0.5 to 1.5
- out_first: float32 [4, 512], P(None, 'chan'), may hold values from -32 to 32
- out_second: float32 [4, 512], P(None, 'chan'), may hold values from 125.44 to 501.76
Outputs:
- block_out: float32 [25088, 512], P('dp', 'chan')
- clip_pool: float32 [128, 512], P('dp', 'chan')
- input_grad: float32 [25088, 512], P('dp', 'chan')
- spatial_new: float32 [2, 4608, 1152], P(None, 'dp', 'chan')
- spatial_first_new: float32 [2, 4608, 1152], P(None, 'dp', 'chan')
- spatial_second_new: float32 [2, 4608, 1152], P(None, 'dp', 'chan')
- temporal_new: float32 [2, 3, 1152, 512], P(None, None, 'chan', 'dp')
- temporal_first_new: float32 [2, 3, 1152, 512], P(None, None, 'chan', 'dp')
- temporal_second_new: float32 [2, 3, 1152, 512], P(None, None, 'chan', 'dp')
- mid_norm_new: float32 [4, 1152], P(None, 'chan')
- mid_first_new: float32 [4, 1152], P(None, 'chan')
- mid_second_new: float32 [4, 1152], P(None, 'chan')
- out_norm_new: float32 [4, 512], P(None, 'chan')
- out_first_new: float32 [4, 512], P(None, 'chan')
- out_second_new: float32 [4, 512], P(None, 'chan')
Inputs may be any that keep to these rules, and one draw needn't show every extreme that they name: Each entry is 8, 16 or 32; a clip keeps its first clip_frames // 8 of 4 frame slots; every draw holds both 8 and 32.
All inputs are finite; a program needn't handle non-finite values.
Results may differ from a plain program's by a relative error of at most 0.025.
Values may be sent and summed in bfloat16 or wider, within the bound.
A program may use at most 320 MiB of HBM per device.

v0:
```python
import jax
import jax.numpy as jnp
from jax import lax
from jax.sharding import PartitionSpec as P

FRAMES = 4
SIDE = 7
STEP = 10
HW = 49


EPS_NORM = 1e-05
EPS_ADAM = 1e-08
BETA_ONE = 0.9
BETA_TWO = 0.95
RATE_CONV = 0.01
RATE_NORM = 0.8
DECAY_CONV = 0.05


def frame_mask(clip_frames):
    kept_frames = clip_frames // 8
    frame_ids = jnp.arange(FRAMES, dtype=jnp.int32)
    frame_grid = (frame_ids[None, :] < kept_frames[:, None]).astype(jnp.float32)
    return jnp.broadcast_to(frame_grid[:, :, None], (kept_frames.shape[0], FRAMES, HW)).reshape(
        -1, 1
    )


def silu_slope(values):
    sigmoid = jax.nn.sigmoid(values)
    return sigmoid * (1.0 + values * (1.0 - sigmoid))


def spatial_apply(inputs, tap_weights):
    channels = inputs.shape[1]
    padded = jnp.pad(inputs.reshape(-1, SIDE, SIDE, channels), ((0, 0), (1, 1), (1, 1), (0, 0)))
    summed = jnp.zeros((inputs.shape[0], tap_weights.shape[2]), jnp.float32)
    for tap_index in range(9):
        row_off, col_off = (tap_index // 3, tap_index % 3)
        window = padded[:, row_off : row_off + SIDE, col_off : col_off + SIDE].reshape(-1, channels)
        summed = summed + jnp.dot(
            window, tap_weights[tap_index], preferred_element_type=jnp.float32
        )
    return (summed, padded)


def spatial_grads(padded, tap_weights, grad_out):
    channels = padded.shape[3]
    weight_terms = []
    input_sum = jnp.zeros((padded.shape[0], SIDE, SIDE, channels), jnp.float32)
    for tap_index in range(9):
        row_off, col_off = (tap_index // 3, tap_index % 3)
        window = padded[:, row_off : row_off + SIDE, col_off : col_off + SIDE].reshape(-1, channels)
        weight_terms.append(
            lax.dot_general(
                window, grad_out, (((0,), (0,)), ((), ())), preferred_element_type=jnp.float32
            )
        )
        pulled = lax.dot_general(
            grad_out,
            tap_weights[tap_index],
            (((1,), (1,)), ((), ())),
            preferred_element_type=jnp.float32,
        )
        pulled = jnp.pad(pulled.reshape(-1, SIDE, SIDE, channels), ((0, 0), (1, 1), (1, 1), (0, 0)))
        input_sum = (
            input_sum
            + pulled[:, 2 - row_off : 2 - row_off + SIDE, 2 - col_off : 2 - col_off + SIDE]
        )
    return (jnp.stack(weight_terms).reshape(-1, grad_out.shape[1]), input_sum.reshape(-1, channels))


def temporal_apply(inputs, weight):
    frame_seq = inputs.reshape(-1, FRAMES, HW, inputs.shape[1])
    padded = jnp.pad(frame_seq, ((0, 0), (1, 1), (0, 0), (0, 0)))
    summed = jnp.zeros(frame_seq.shape[:3] + (weight.shape[2],), jnp.float32)
    for frame_off in range(3):
        summed = summed + jnp.einsum(
            "nfpm,mc->nfpc",
            padded[:, frame_off : frame_off + FRAMES],
            weight[frame_off],
            preferred_element_type=jnp.float32,
        )
    return (summed.reshape(inputs.shape[0], -1), padded)


def temporal_grads(padded, weight, grad_full):
    grad_seq = grad_full.reshape(-1, FRAMES, HW, grad_full.shape[1])
    grad_pad = jnp.pad(grad_seq, ((0, 0), (1, 1), (0, 0), (0, 0)))
    weight_terms = []
    input_sum = jnp.zeros(padded.shape[:1] + (FRAMES, HW, padded.shape[3]), jnp.float32)
    for frame_off in range(3):
        weight_terms.append(
            jnp.einsum(
                "nfpm,nfpc->mc",
                padded[:, frame_off : frame_off + FRAMES],
                grad_seq,
                preferred_element_type=jnp.float32,
            )
        )
        input_sum = input_sum + jnp.einsum(
            "nfpc,mc->nfpm",
            grad_pad[:, 2 - frame_off : 2 - frame_off + FRAMES],
            weight[frame_off],
            preferred_element_type=jnp.float32,
        )
    return (jnp.stack(weight_terms), input_sum.reshape(grad_full.shape[0], -1))


def normalize(values, validity, gain_row, bias_row):
    local_valid = jnp.sum(validity)
    total_valid, value_sums = lax.psum((local_valid, jnp.sum(values * validity, axis=0)), "dp")
    average = value_sums / total_valid
    centered = values - average
    variance = lax.psum(jnp.sum(validity * centered * centered, axis=0), "dp") / total_valid
    inverse = lax.rsqrt(variance + EPS_NORM)
    standard = centered * inverse
    return (standard * gain_row + bias_row, standard, inverse, total_valid)


def normalize_back(grad_normed, standard, inverse, gain_row, total_valid, validity):
    grad_bias, grad_gain = lax.psum(
        (
            jnp.sum(grad_normed * validity, axis=0),
            jnp.sum(grad_normed * standard * validity, axis=0),
        ),
        "dp",
    )
    grad_values = (
        validity
        * gain_row
        * inverse
        * (grad_normed - grad_bias / total_valid - standard * grad_gain / total_valid)
    )
    return (grad_values, grad_gain, grad_bias)


def adam_update(weight, moment_one, moment_two, grad_value, rate, decay):
    fresh_one = BETA_ONE * moment_one + (1.0 - BETA_ONE) * grad_value
    fresh_two = BETA_TWO * moment_two + (1.0 - BETA_TWO) * grad_value * grad_value
    scaled = (
        fresh_one
        / (1.0 - BETA_ONE**STEP)
        / (jnp.sqrt(fresh_two / (1.0 - BETA_TWO**STEP)) + EPS_ADAM)
    )
    return (weight - rate * (scaled + decay * weight), fresh_one, fresh_two)


def on_device(
    features,
    cotangent,
    clip_frames,
    spatial_master,
    spatial_first,
    spatial_second,
    temporal_master,
    temporal_first,
    temporal_second,
    mid_norm,
    mid_first,
    mid_second,
    out_norm,
    out_first,
    out_second,
):
    validity = frame_mask(clip_frames)
    spatial_all, temporal_all = (
        lax.all_gather(spatial_master.astype(jnp.bfloat16), "dp", axis=1, tiled=True),
        lax.all_gather(temporal_master.astype(jnp.bfloat16), "dp", axis=3, tiled=True),
    )
    channels = temporal_all.shape[3]
    spatial_taps = spatial_all.reshape(2, 9, channels, spatial_all.shape[2])
    residual = features.astype(jnp.float32)
    outgoing = features
    kept_state = []
    for unit_index in range(2):
        gathered = lax.all_gather(outgoing, "chan", axis=1, tiled=True)
        spatial_out, padded = spatial_apply(gathered, spatial_taps[unit_index])
        mid_normed, mid_standard, mid_inverse, total_valid = normalize(
            spatial_out, validity, mid_norm[2 * unit_index], mid_norm[2 * unit_index + 1]
        )
        temporal_in = (jax.nn.silu(mid_normed) * validity).astype(jnp.bfloat16)
        partial_value, frames_padded = temporal_apply(temporal_in, temporal_all[unit_index])
        temporal_out = lax.psum_scatter(
            partial_value.astype(jnp.bfloat16), "chan", scatter_dimension=1, tiled=True
        ).astype(jnp.float32)
        out_normed, out_standard, out_inverse, total_valid = normalize(
            temporal_out, validity, out_norm[2 * unit_index], out_norm[2 * unit_index + 1]
        )
        if unit_index == 0:
            pre_act = out_normed
            outgoing = (jax.nn.silu(pre_act) * validity).astype(jnp.bfloat16)
        else:
            pre_act = out_normed + residual
            block_out = jax.nn.silu(pre_act) * validity
        kept_state.append(
            (
                padded,
                mid_normed,
                mid_standard,
                mid_inverse,
                frames_padded,
                pre_act,
                out_standard,
                out_inverse,
            )
        )
    kept_frames = (clip_frames // 8).astype(jnp.float32)
    clip_pool = (
        jnp.sum(block_out.reshape(-1, FRAMES * HW, block_out.shape[1]), axis=1)
        / (HW * kept_frames)[:, None]
    )
    skip_grad = cotangent * validity * silu_slope(kept_state[1][5])
    grad_pre = skip_grad
    spatial_list = [None, None]
    temporal_list = [None, None]
    mid_rows = [None, None]
    out_rows = [None, None]
    grad_hidden = skip_grad
    for unit_index in (1, 0):
        (
            padded,
            mid_normed,
            mid_standard,
            mid_inverse,
            frames_padded,
            pre_act,
            out_standard,
            out_inverse,
        ) = kept_state[unit_index]
        if unit_index == 0:
            grad_pre = grad_hidden * validity * silu_slope(pre_act)
        grad_temporal, out_gain_grad, out_bias_grad = normalize_back(
            grad_pre, out_standard, out_inverse, out_norm[2 * unit_index], total_valid, validity
        )
        grad_full = lax.all_gather(grad_temporal.astype(jnp.bfloat16), "chan", axis=1, tiled=True)
        temporal_grad, grad_mid = temporal_grads(frames_padded, temporal_all[unit_index], grad_full)
        grad_mid_normed = grad_mid * validity * silu_slope(mid_normed)
        grad_spatial, mid_gain_grad, mid_bias_grad = normalize_back(
            grad_mid_normed,
            mid_standard,
            mid_inverse,
            mid_norm[2 * unit_index],
            total_valid,
            validity,
        )
        spatial_grad, grad_in_part = spatial_grads(
            padded, spatial_taps[unit_index], grad_spatial.astype(jnp.bfloat16)
        )
        grad_hidden = lax.psum_scatter(
            grad_in_part.astype(jnp.bfloat16), "chan", scatter_dimension=1, tiled=True
        ).astype(jnp.float32)
        spatial_list[unit_index] = spatial_grad
        temporal_list[unit_index] = temporal_grad
        mid_rows[unit_index] = (mid_gain_grad, mid_bias_grad)
        out_rows[unit_index] = (out_gain_grad, out_bias_grad)
    input_grad = grad_hidden + skip_grad
    spatial_sum, temporal_sum = (
        lax.psum_scatter(jnp.stack(spatial_list), "dp", scatter_dimension=1, tiled=True),
        lax.psum_scatter(jnp.stack(temporal_list), "dp", scatter_dimension=3, tiled=True),
    )
    mid_grad = jnp.stack([mid_rows[0][0], mid_rows[0][1], mid_rows[1][0], mid_rows[1][1]])
    out_grad = jnp.stack([out_rows[0][0], out_rows[0][1], out_rows[1][0], out_rows[1][1]])
    spatial_new, spatial_one, spatial_two = adam_update(
        spatial_master, spatial_first, spatial_second, spatial_sum, RATE_CONV, DECAY_CONV
    )
    temporal_new, temporal_one, temporal_two = adam_update(
        temporal_master, temporal_first, temporal_second, temporal_sum, RATE_CONV, DECAY_CONV
    )
    mid_new, mid_one, mid_two = adam_update(
        mid_norm, mid_first, mid_second, mid_grad, RATE_NORM, 0.0
    )
    out_new, out_one, out_two = adam_update(
        out_norm, out_first, out_second, out_grad, RATE_NORM, 0.0
    )
    return (
        block_out,
        clip_pool,
        input_grad,
        spatial_new,
        spatial_one,
        spatial_two,
        temporal_new,
        temporal_one,
        temporal_two,
        mid_new,
        mid_one,
        mid_two,
        out_new,
        out_one,
        out_two,
    )


def solution(mesh):
    in_specs = (
        P("dp", "chan"),
        P("dp", "chan"),
        P("dp"),
        P(None, "dp", "chan"),
        P(None, "dp", "chan"),
        P(None, "dp", "chan"),
        P(None, None, "chan", "dp"),
        P(None, None, "chan", "dp"),
        P(None, None, "chan", "dp"),
        P(None, "chan"),
        P(None, "chan"),
        P(None, "chan"),
        P(None, "chan"),
        P(None, "chan"),
        P(None, "chan"),
    )
    out_specs = (
        P("dp", "chan"),
        P("dp", "chan"),
        P("dp", "chan"),
        P(None, "dp", "chan"),
        P(None, "dp", "chan"),
        P(None, "dp", "chan"),
        P(None, None, "chan", "dp"),
        P(None, None, "chan", "dp"),
        P(None, None, "chan", "dp"),
        P(None, "chan"),
        P(None, "chan"),
        P(None, "chan"),
        P(None, "chan"),
        P(None, "chan"),
        P(None, "chan"),
    )
    return jax.shard_map(
        on_device, mesh=mesh, in_specs=in_specs, out_specs=out_specs, check_vma=False
    )
```

profile of v0, /device:TPU:0, one launch (start us, length us, event | category | flops | bytes accessed | tf_op | source)
XLA Modules:
  0.0 1442.9 jit_solution(3506100995256527197)
XLA Ops:
  16.0 26.2 %all-gather.11.cloned.1.call-done = bf16[2,3,288,512]{2,0,1,3:T(2,128)(2,1)} async-done(((bf16[2,3,288,64]{2,0,1,3:T(2,128)(2,1)}), bf16[2,3,288,512]{2,0,1,3:T(2,128)(2,1)}) %all-gather.11.cloned.1.call-update) | async-done | bytes 1769488 | tf_op jit(solution)/shard_map/all_gather | solution.py:170
  42.2 6.6 fusion.209
  54.5 53.8 %all-gather.7.cloned.1.call-done = bf16[3136,512]{1,0:T(8,128)(2,1)} async-done(((bf16[3136,128]{1,0:T(8,128)(2,1)}), bf16[3136,512]{1,0:T(8,128)(2,1)}) %all-gather.7.cloned.1.call-update) | async-done | bytes 3211280 | tf_op jit(solution)/shard_map/all_gather | solution.py:178
  108.4 6.1 reshape.265
  114.5 22.3 %pad_slice_fusion.8 = (bf16[64,7,7,512]{3,2,1,0:T(8,128)(2,1)}, bf16[64,7,7,512]{3,2,1,0:T(8,128)(2,1)}, bf16[64,7,7,512]{3,2,1,0:T(8,128)(2,1)}, bf16[64,7,7,51...) fusion(bf16[64,7,7,512]{3,2,1,0:T(8,128)(2,1)} %reshape.265), kind=kLoop, calls=%fused_computation.8 | loop fusion | bytes 28901376 | tf_op jit(solution)/shard_map/slice | solution.py:41
  141.6 6.5 reshape.267
  148.1 6.1 reshape.268
  154.2 6.2 reshape.269
  160.3 6.1 reshape.270
  166.5 6.1 reshape.271
  172.6 6.1 reshape.272
  178.7 6.1 reshape.266
  184.9 18.4 %fusion.208 = (bf16[1,512,288]{2,0,1:T(2,128)(2,1)}, bf16[1,512,288]{2,0,1:T(2,128)(2,1)}, bf16[1,512,288]{2,0,1:T(2,128)(2,1)}, bf16[1,512,288]{2,0,1:T(2,128)(...) fusion(bf16[2,4608,288]{2,0,1:T(2,128)(2,1)} %all-gather.9.clon, ...), kind=kLoop, calls=%fused_computation.319 | loop fusion | bytes 10616832 | tf_op jit(solution)/shard_map/slice | solution.py:43
  247.5 14.4 all-reduce.27
  265.2 12.2 psum.130
  303.1 58.1 %reduce-scatter.16.cloned.1.call-done = bf16[128,3136]{1,0:T(8,128)(2,1)} async-done(((bf16[512,3136]{1,0:T(8,128)(2,1)}), bf16[128,3136]{1,0:T(8,128)(2,1)}) %reduce-scatter.16.cloned.1.call-update) | async-done | bytes 802832
  363.8 13.6 psum.131
  378.5 11.8 psum.132
  420.7 35.7 %all-gather.13.cloned.1.call-done = bf16[3136,512]{1,0:T(8,128)(2,1)} async-done(((bf16[3136,128]{1,0:T(8,128)(2,1)}), bf16[3136,512]{1,0:T(8,128)(2,1)}) %all-gather.13.cloned.1.call-update) | async-done | bytes 3211280 | tf_op jit(solution)/shard_map/all_gather | solution.py:178
  456.3 6.1 reshape.275
  462.4 21.3 %pad_slice_fusion = (bf16[64,7,7,512]{3,2,1,0:T(8,128)(2,1)}, bf16[64,7,7,512]{3,2,1,0:T(8,128)(2,1)}, bf16[64,7,7,512]{3,2,1,0:T(8,128)(2,1)}, bf16[64,7,7,512]...) fusion(bf16[64,7,7,512]{3,2,1,0:T(8,128)(2,1)} %reshape.275), kind=kLoop, calls=%fused_computation | loop fusion | bytes 28901376 | tf_op jit(solution)/shard_map/slice | solution.py:41
  488.6 6.4 reshape.277
  495.0 6.1 reshape.278
  501.1 6.1 reshape.279
  507.2 6.1 reshape.280
  513.4 6.1 reshape.281
  519.5 6.1 reshape.282
  525.6 6.3 reshape.276
  551.1 13.9 psum.133
  568.4 12.2 psum.134
  607.0 58.7 %reduce-scatter.18.cloned.1.call-done = bf16[128,3136]{1,0:T(8,128)(2,1)} async-done(((bf16[512,3136]{1,0:T(8,128)(2,1)}), bf16[128,3136]{1,0:T(8,128)(2,1)}) %reduce-scatter.18.cloned.1.call-update) | async-done | bytes 802832
  668.2 13.4 psum.135
  682.7 11.8 psum.136
  699.4 11.9 all-reduce.26
  714.8 63.1 %all-gather.15.cloned.1.call-done = bf16[3136,512]{1,0:T(8,128)(2,1)} async-done(((bf16[3136,128]{1,0:T(8,128)(2,1)}), bf16[3136,512]{1,0:T(8,128)(2,1)}) %all-gather.15.cloned.1.call-update) | async-done | bytes 3211280 | tf_op jit(solution)/shard_map/all_gather | solution.py:237
  777.9 4.9 reshape.286
  794.0 5.3 reshape.287
  799.4 5.8 copy.402
  805.1 6.2 multiply_reduce_fusion.3
  811.3 13.8 all-reduce.25
  838.3 5.8 fusion.138
  871.4 5.1 fusion.140
  876.4 19.7 %add_convert_fusion.3 = bf16[64,7,7,512]{3,0,2,1:T(8,128)(2,1)} fusion(f32[64,7,7,512]{3,0,2,1:T(8,128)} %fusion.126, f32[64,7,7,512]{3,0,2,1:T(8,128)} %fusion.128, f32[64,7,7,512]{3,0,2,1:T(8,128)} %fusion.130, f32[64,7,7,512]{3,0,2,1:T(8,128)} %fusion.132, f32[64,7,7,512]{3,0,2,1:T(8,128)} %fusion.134, f32[64,7,7,512]{3,0,2,1:T(8,128)} %fusion.136, ...), kind=kOutput, calls=%fused_computation.20 | convolution fusion | flops 693927936 | bytes 56692736 | tf_op jit(solution)/shard_map/slice | solution.py:69
  896.1 5.7 copy.413
  910.5 58.7 %reduce-scatter.20.cloned.1.call-done = bf16[128,3136]{1,0:T(8,128)(2,1)} async-done(((bf16[512,3136]{1,0:T(8,128)(2,1)}), bf16[128,3136]{1,0:T(8,128)(2,1)}) %reduce-scatter.20.cloned.1.call-update) | async-done | bytes 802832
  975.4 14.1 all-reduce.24
  1015.1 42.7 %all-gather.17.cloned.1.call-done = bf16[3136,512]{1,0:T(8,128)(2,1)} async-done(((bf16[3136,128]{1,0:T(8,128)(2,1)}), bf16[3136,512]{1,0:T(8,128)(2,1)}) %all-gather.17.cloned.1.call-update) | async-done | bytes 3211280 | tf_op jit(solution)/shard_map/all_gather | solution.py:237
  1057.8 4.9 reshape.288
  1071.3 4.9 add_add_fusion
  1076.2 5.4 reshape.289
  1081.6 5.8 copy.414
  1087.4 6.2 multiply_reduce_fusion.1
  1093.6 13.8 all-reduce.23
  1152.4 4.9 fusion.123
  1163.6 7.6 copy.444
  1172.1 21.0 %add_convert_fusion.2 = bf16[64,7,7,512]{3,0,2,1:T(8,128)(2,1)} fusion(f32[64,7,7,512]{3,0,2,1:T(8,128)} %fusion.109, f32[64,7,7,512]{3,0,2,1:T(8,128)} %fusion.111, f32[64,7,7,512]{3,0,2,1:T(8,128)} %fusion.113, f32[64,7,7,512]{3,0,2,1:T(8,128)} %fusion.115, f32[64,7,7,512]{3,0,2,1:T(8,128)} %fusion.117, f32[64,7,7,512]{3,0,2,1:T(8,128)} %fusion.119, ...), kind=kOutput, calls=%fused_computation.19 | convolution fusion | flops 693927936 | bytes 56692736 | tf_op jit(solution)/shard_map/slice | solution.py:69
  1193.1 5.7 copy.425
  1198.8 5.0 convert_element_type.126
  1221.1 7.0 copy.428
  1248.3 6.7 copy.427
  1255.0 11.2 pad_maximum_fusion
  1284.5 34.8 %reduce-scatter.22.cloned.1.call-done = bf16[128,3136]{1,0:T(8,128)(2,1)} async-done(((bf16[512,3136]{1,0:T(8,128)(2,1)}), bf16[128,3136]{1,0:T(8,128)(2,1)}) %reduce-scatter.22.cloned.1.call-update) | async-done | bytes 802832
  1323.9 100.2 %reduce-scatter.14.cloned.1.call-done = f32[2,576,288]{2,1,0:T(8,128)} async-done(((f32[2,4608,288]{2,1,0:T(8,128)}), f32[2,576,288]{2,1,0:T(8,128)}) %reduce-scatter.14.cloned.1.call-update) | async-done | bytes 1327120 | tf_op jit(solution)/shard_map/reduce_scatter | solution.py:260
  1424.0 5.7 multiply_subtract_fusion
  (495 shorter events, 409.4 us)
Async XLA Ops:
  7.2 6.7 copy-start.147
  7.2 7.5 copy-start.121
  7.2 35.0 %all-gather.11.cloned.1.call-start = ((), (), s32[]{:S(2)}) async-start(), calls=%async_computation.7 | async-start | bytes 2654208 | tf_op jit(solution)/shard_map/all_gather | solution.py:170
  9.5 98.9 %all-gather.7.cloned.1.call-start = ((), (), s32[]{:S(2)}) async-start(), calls=%async_computation.5 | async-start | bytes 4014080 | tf_op jit(solution)/shard_map/all_gather | solution.py:178
  10.3 174.6 %all-gather.9.cloned.1.call-start = ((), (), s32[]{:S(2)}) async-start(), calls=%async_computation.6 | async-start | bytes 7962624 | tf_op jit(solution)/shard_map/all_gather | solution.py:169
  13.8 347.5 %reduce-scatter.16.cloned.1.call-start = ((), (), s32[]{:S(2)}) async-start(), calls=%async_computation.12 | async-start | bytes 4096000
  14.7 811.1 %copy-start.46 = (f32[3136]{0:T(1024)}, f32[3136]{0:T(1024)S(1)}, u32[]{:S(2)}) copy-start(f32[3136]{0:T(1024)S(1)} %mul.547) | copy-start | bytes 37636
  15.3 262.7 %copy-start.116 = (f32[288]{0:T(512)}, f32[288]{0:T(512)S(1)}, u32[]{:S(2)}) copy-start(f32[288]{0:T(512)S(1)} %get-tuple-element.115) | copy-start | bytes 3460
  15.3 262.7 %copy-start.123 = (f32[288]{0:T(512)}, f32[288]{0:T(512)S(1)}, u32[]{:S(2)}) copy-start(f32[288]{0:T(512)S(1)} %get-tuple-element.114) | copy-start | bytes 3460
  141.6 102.9 %copy-start.12 = (bf16[3136,512]{1,0:T(8,128)(2,1)}, bf16[3136,512]{1,0:T(8,128)(2,1)S(1)}, u32[]{:S(2)}) copy-start(bf16[3136,512]{1,0:T(8,128)(2,1)S(1)} %reshape.273) | copy-start | bytes 9633796
  205.5 39.0 %copy-start.68 = (bf16[1,512,288]{1,2,0:T(8,128)(2,1)}, bf16[1,512,288]{1,2,0:T(8,128)(2,1)S(1)}, u32[]{:S(2)}) copy-start(bf16[1,512,288]{1,2,0:T(8,128)(2,1)S(1)} %copy.498) | copy-start | bytes 884740
  262.5 19.2 %copy-start.114 = (f32[288]{0:T(512)}, f32[288]{0:T(512)S(1)}, u32[]{:S(2)}) copy-start(f32[288]{0:T(512)S(1)} %broadcast_divide_fusion.4) | copy-start | bytes 3460
  302.5 90.7 %copy-start.65 = (bf16[1,1,288,512]{2,0,1,3:T(2,128)(2,1)S(1)}, bf16[1,1,288,512]{2,0,1,3:T(2,128)(2,1)}, u32[]{:S(2)}) copy-start(bf16[1,1,288,512]{2,0,1,3:T(2,128)(2,1)} %get-tuple-element.183) | copy-start | bytes 884740
  302.5 153.9 %all-gather.13.cloned.1.call-start = ((), (), s32[]{:S(2)}) async-start(), calls=%async_computation.8 | async-start | bytes 4014080 | tf_op jit(solution)/shard_map/all_gather | solution.py:178
  303.1 92.2 %copy-start.131 = (f32[128]{0:T(128)}, f32[128]{0:T(128)S(1)}, u32[]{:S(2)}) copy-start(f32[128]{0:T(128)S(1)} %get-tuple-element.192) | copy-start | bytes 1540
  303.1 92.2 %copy-start.136 = (f32[128]{0:T(128)}, f32[128]{0:T(128)S(1)}, u32[]{:S(2)}) copy-start(f32[128]{0:T(128)S(1)} %get-tuple-element.191) | copy-start | bytes 1540
  361.3 34.0 %copy-start.64 = (bf16[1,1,288,512]{2,0,1,3:T(2,128)(2,1)S(1)}, bf16[1,1,288,512]{2,0,1,3:T(2,128)(2,1)}, u32[]{:S(2)}) copy-start(bf16[1,1,288,512]{2,0,1,3:T(2,128)(2,1)} %get-tuple-element.184) | copy-start | bytes 884740
  363.3 35.8 %copy-start.8 = (bf16[3136,128]{1,0:T(8,128)(2,1)}, bf16[3136,128]{1,0:T(8,128)(2,1)S(1)}, u32[]{:S(2)}) copy-start(bf16[3136,128]{1,0:T(8,128)(2,1)S(1)} %copy.482) | copy-start | bytes 2408452
  363.3 33.9 %copy-start.63 = (bf16[1,1,288,512]{2,0,1,3:T(2,128)(2,1)S(1)}, bf16[1,1,288,512]{2,0,1,3:T(2,128)(2,1)}, u32[]{:S(2)}) copy-start(bf16[1,1,288,512]{2,0,1,3:T(2,128)(2,1)} %get-tuple-element.185) | copy-start | bytes 884740
  378.0 21.1 %copy-start.130 = (f32[128]{0:T(128)}, f32[128]{0:T(128)S(1)}, u32[]{:S(2)}) copy-start(f32[128]{0:T(128)S(1)} %broadcast_divide_fusion.8) | copy-start | bytes 1540
  391.0 10.6 copy-start.137
  393.2 272.5 %reduce-scatter.18.cloned.1.call-start = ((), (), s32[]{:S(2)}) async-start(), calls=%async_computation.13 | async-start | bytes 4096000
  397.3 15.8 %copy-start.62 = (bf16[1,512,288]{2,0,1:T(2,128)(2,1)S(1)}, bf16[1,512,288]{2,0,1:T(2,128)(2,1)}, u32[]{:S(2)}) copy-start(bf16[1,512,288]{2,0,1:T(2,128)(2,1)} %get-tuple-element.150) | copy-start | bytes 884740
  399.2 15.8 %copy-start.61 = (bf16[1,512,288]{2,0,1:T(2,128)(2,1)S(1)}, bf16[1,512,288]{2,0,1:T(2,128)(2,1)}, u32[]{:S(2)}) copy-start(bf16[1,512,288]{2,0,1:T(2,128)(2,1)} %get-tuple-element.151) | copy-start | bytes 884740
  401.5 15.3 %copy-start.60 = (bf16[1,512,288]{2,0,1:T(2,128)(2,1)S(1)}, bf16[1,512,288]{2,0,1:T(2,128)(2,1)}, u32[]{:S(2)}) copy-start(bf16[1,512,288]{2,0,1:T(2,128)(2,1)} %get-tuple-element.152) | copy-start | bytes 884740
  404.5 14.3 copy-start.59
  488.5 59.4 %copy-start.28 = (bf16[3136,512]{1,0:T(8,128)(2,1)}, bf16[3136,512]{1,0:T(8,128)(2,1)S(1)}, u32[]{:S(2)}) copy-start(bf16[3136,512]{1,0:T(8,128)(2,1)S(1)} %reshape.283) | copy-start | bytes 9633796
  551.1 30.1 %copy-start.118 = (f32[288]{0:T(512)S(1)}, f32[288]{0:T(512)}, u32[]{:S(2)}) copy-start(f32[288]{0:T(512)} %get-tuple-element.113) | copy-start | bytes 3460
  551.1 30.1 %copy-start.125 = (f32[288]{0:T(512)S(1)}, f32[288]{0:T(512)}, u32[]{:S(2)}) copy-start(f32[288]{0:T(512)} %get-tuple-element.116) | copy-start | bytes 3460
  590.3 5.5 copy-start.2
  606.9 88.3 %copy-start.58 = (bf16[3136,128]{1,0:T(8,128)(2,1)S(1)}, bf16[3136,128]{1,0:T(8,128)(2,1)}, u32[]{:S(2)}) copy-start(bf16[3136,128]{1,0:T(8,128)(2,1)} %param.15) | copy-start | bytes 2408452
  606.9 171.0 %all-gather.15.cloned.1.call-start = ((), (), s32[]{:S(2)}) async-start(), calls=%async_computation.9 | async-start | bytes 4014080 | tf_op jit(solution)/shard_map/all_gather | solution.py:237
  699.4 83.5 %copy-start.44 = (f32[3136,128]{1,0:T(8,128)}, f32[3136,128]{1,0:T(8,128)S(1)}, u32[]{:S(2)}) copy-start(f32[3136,128]{1,0:T(8,128)S(1)} %get-tuple-element.142) | copy-start | bytes 4816900
  711.3 66.6 %copy-start.144 = (f32[128]{0:T(128)}, f32[128]{0:T(128)S(1)}, u32[]{:S(2)}) copy-start(f32[128]{0:T(128)S(1)} %get-tuple-element.124) | copy-start | bytes 1540
  711.3 71.6 %copy-start.140 = (f32[128]{0:T(128)}, f32[128]{0:T(128)S(1)}, u32[]{:S(2)}) copy-start(f32[128]{0:T(128)S(1)} %get-tuple-element.123) | copy-start | bytes 1540
  714.8 68.1 %copy-start.105 = (bf16[1,1,288,512]{3,2,1,0:T(8,128)(2,1)S(1)}, bf16[1,1,288,512]{3,2,1,0:T(8,128)(2,1)}, u32[]{:S(2)}) copy-start(bf16[1,1,288,512]{3,2,1,0:T(8,128)(2,1)} %copy.511) | copy-start | bytes 884740
  714.8 254.4 %reduce-scatter.20.cloned.1.call-start = ((), (), s32[]{:S(2)}) async-start(), calls=%async_computation.14 | async-start | bytes 4096000
  825.1 5.3 copy-start.132
  838.3 5.9 copy-start.101
  910.4 60.9 %copy-start.9 = (bf16[3136,128]{1,0:T(8,128)(2,1)S(1)}, bf16[3136,128]{1,0:T(8,128)(2,1)}, u32[]{:S(2)}) copy-start(bf16[3136,128]{1,0:T(8,128)(2,1)} %copy-done.8) | copy-start | bytes 2408452
  910.4 147.4 %all-gather.17.cloned.1.call-start = ((), (), s32[]{:S(2)}) async-start(), calls=%async_computation.10 | async-start | bytes 4014080 | tf_op jit(solution)/shard_map/all_gather | solution.py:237
  971.3 23.3 %copy-start.1 = (bf16[16,4,49,288]{3,2,1,0:T(8,128)(2,1)S(1)}, bf16[16,4,49,288]{3,2,1,0:T(8,128)(2,1)}, u32[]{:S(2)}) copy-start(bf16[16,4,49,288]{3,2,1,0:T(8,128)(2,1)} %copy-done) | copy-start | bytes 5419012
  994.6 285.5 %all-reduce.30.cloned.1.call-start = ((), (), s32[]{:S(2)}) async-start(), calls=%async_computation.16 | async-start | bytes 9437184
  1081.6 5.8 copy-start.47
  1081.6 5.8 copy-start.115
  1081.6 5.8 copy-start.117
  1081.6 5.8 copy-start.120
  1081.6 5.8 copy-start.124
  1152.4 4.9 copy-start.7
  1152.4 4.9 copy-start.67
  1171.2 148.1 %reduce-scatter.22.cloned.1.call-start = ((), (), s32[]{:S(2)}) async-start(), calls=%async_computation.15 | async-start | bytes 4096000
  1207.5 216.6 %reduce-scatter.14.cloned.1.call-start = ((), (), s32[]{:S(2)}) async-start(), calls=%async_computation.11 | async-start | bytes 15925248 | tf_op jit(solution)/shard_map/reduce_scatter | solution.py:260
  1221.1 7.0 copy-start.42
  1268.4 5.6 copy-start.148
  1268.4 6.9 copy-start.55
  1273.9 4.9 copy-start.127
  1273.9 4.9 copy-start.138
  1273.9 4.9 copy-start.139
  1273.9 4.9 copy-start.141
  1274.0 4.9 copy-start.142
  1274.0 5.5 copy-start.122
  1274.0 5.5 copy-start.134
  1274.0 5.5 copy-start.135
  1280.1 41.3 %copy-start.45 = (f32[3136,128]{1,0:T(8,128)S(1)}, f32[3136,128]{1,0:T(8,128)}, u32[]{:S(2)}) copy-start(f32[3136,128]{1,0:T(8,128)} %copy-done.44) | copy-start | bytes 4816900
  (97 other events, 265.9 us)
Sparse Core Ops, SparseCore 0:
  10.5 31.7 all-gather.10
  43.8 64.5 all-gather.6
  110.8 46.9 all-gather.8
  302.6 58.6 reduce-scatter.15
  393.3 62.9 all-gather.12
  607.1 58.6 reduce-scatter.17
  714.9 62.9 all-gather.14
  910.5 58.5 reduce-scatter.19
  994.7 62.9 all-gather.16
  1171.3 83.1 all-reduce.29
  1256.9 62.3 reduce-scatter.21
  1323.1 100.8 reduce-scatter.13
where the time goes:
time: 1460 us; the launch traced here: 1440 us
  waiting for transfers between devices  533 us (37%)
  local copies, waits for them, and re-layouts  411 us (28%)
  matrix products  232 us (16%)
  blocking collectives  157 us (11%)
  other arithmetic  92.8 us (6%)
  between operations  16.6 us (1%)
    unnamed x17, waiting for transfers between devices  211 us
    unnamed x339, local copies, waits for them, and re-layouts  122 us
    slice x16, matrix products, spatial_grads(): pulled[:, 2 - row_off:2 - row_off + SIDE, 2 - col_off:2 - col_off + SIDE]  106 us
    all_gather x2, waiting for transfers between devices, on_device(): lax.all_gather(grad_temporal.astype(jnp.bfloat16), 'chan', axis=1, tiled=...  106 us
    reduce_scatter x1, waiting for transfers between devices, on_device(): lax.psum_scatter(jnp.stack(spatial_list), 'dp', scatter_dimension=1, tile...  100 us
    reshape x16, local copies, waits for them, and re-layouts, spatial_apply(): padded[:, row_off:row_off + SIDE, col_off:col_off + SIDE]  96.1 us
    all_gather x2, waiting for transfers between devices, on_device(): gathered = lax.all_gather(outgoing, 'chan', axis=1, tiled=True)  89.5 us
    psum x4, blocking collectives, normalize(): lax.psum((local_valid, jnp.sum(values * validity, axis=0)), 'dp')  55.3 us
  transfers between devices with their start and end apart: 12, of which 10 were waited for; matrix products, arithmetic and copies ran while one was open for 17% of the time, Pallas kernels for 0%

commit v1 on v0

--- a/solution.py
+++ b/solution.py
@@ -1,6 +1,9 @@
 import jax
 import jax.numpy as jnp
+import numpy as np
 from jax import lax
+from jax.experimental import pallas as pl
+from jax.experimental.pallas import tpu as pltpu
 from jax.sharding import PartitionSpec as P
 
 FRAMES = 4
@@ -293,6 +296,1260 @@
     )
 
 
+F32 = jnp.float32
+BF16 = jnp.bfloat16
+MESH = pl.DeviceIdType.MESH
+VMEM = pltpu.VMEM
+NN = (((1,), (0,)), ((), ()))
+NT = (((1,), (1,)), ((), ()))
+TN = (((0,), (0,)), ((), ()))
+BLOCK_C = 512
+MID_C = 1152
+ROWS = 784
+SLOTS = 16
+HALF = 144
+TAPS_C = 9 * BLOCK_C
+CHIP_S = TAPS_C // 4
+CHIP_T = BLOCK_C // 4
+PARTS = (("s", 0), ("t", 0), ("s", 1), ("t", 1))
+GRANT = 62 * 1024 * 1024
+
+
+def place():
+    dp = lax.axis_index("dp")
+    line = lax.axis_index("chan")
+    core = lax.rem(dp, 2)
+    chip = lax.div(dp, 2)
+    x_bit = lax.rem(chip, 2)
+    y_bit = lax.div(chip, 2)
+    return dict(
+        dp=dp,
+        line=line,
+        core=core,
+        chip=chip,
+        chip_x=chip + 1 - 2 * x_bit,
+        chip_y=chip + 2 - 4 * y_bit,
+        chip_d=3 - chip,
+        pair=(dp + 1 - 2 * core, line),
+        x=(dp + 2 - 4 * x_bit, line),
+        y=(dp + 4 - 8 * y_bit, line),
+    )
+
+
+def remote(source, target, send, recv, device):
+    return pltpu.make_async_remote_copy(
+        src_ref=source,
+        dst_ref=target,
+        send_sem=send,
+        recv_sem=recv,
+        device_id=device,
+        device_id_type=MESH,
+    )
+
+
+def greet(devices):
+    barrier = pltpu.get_barrier_semaphore()
+    for device in devices:
+        pl.semaphore_signal(barrier, inc=1, device_id=device, device_id_type=MESH)
+    pl.semaphore_wait(barrier, len(devices))
+
+
+def line_peer(at, step):
+    return (at["dp"], lax.rem(at["line"] + step, 4))
+
+
+def gather_kernel(
+    ws_in,
+    wt_in,
+    feat_in,
+    cot_in,
+    par_in,
+    ws_out,
+    wt_out,
+    feat_out,
+    cot_out,
+    par_out,
+    pair_s,
+    pair_t,
+    stage_s,
+    stage_t,
+    pair_send,
+    pair_recv,
+    act_send,
+    act_recv,
+    line_send,
+    line_recv,
+    plane_send,
+    plane_recv,
+    diag_send,
+    diag_recv,
+    core_send,
+    core_recv,
+    own_sem,
+):
+    at = place()
+    line, core, chip = at["line"], at["core"], at["chip"]
+    greet([at["pair"], at["x"], at["y"]] + [line_peer(at, step) for step in (1, 2, 3)])
+
+    def area(part, owner_core, owner_chip, first, count):
+        kind, unit = part
+        lines = pl.ds(first, count)
+        if kind == "s":
+            lanes = pl.ds(pl.multiple_of(owner_chip * CHIP_S, 128), CHIP_S)
+            return ws_out.at[unit, lines, owner_core, :, lanes]
+        lanes = pl.ds(pl.multiple_of(owner_chip * CHIP_T, 128), CHIP_T)
+        return wt_out.at[unit, :, lines, owner_core, :, lanes]
+
+    started = []
+
+    def send(copy):
+        copy.start()
+        started.append(copy)
+
+    for index, (kind, unit) in enumerate(PARTS):
+        theirs = pl.ds(pl.multiple_of((1 - core) * HALF, 16), HALF)
+        source, landing = (ws_in, pair_s) if kind == "s" else (wt_in, pair_t)
+        send(
+            remote(
+                source.at[unit, theirs],
+                landing.at[unit],
+                pair_send.at[index],
+                pair_recv.at[index],
+                at["pair"],
+            )
+        )
+
+    def acts(row, source, target, count):
+        def cut(owner):
+            return source.at[pl.ds(pl.multiple_of(owner * count, 16), count)]
+
+        lanes = pl.ds(pl.multiple_of(line * 128, 128), 128)
+        for step in (1, 2, 3):
+            peer = line_peer(at, step)
+            send(
+                remote(
+                    cut(peer[1]),
+                    target.at[:, lanes],
+                    act_send.at[row, step - 1],
+                    act_recv.at[row, step - 1],
+                    peer,
+                )
+            )
+        own = pltpu.make_async_copy(cut(line), target.at[:, lanes], own_sem.at[row])
+        own.start()
+        return own
+
+    def acts_wait(row, source, target, count):
+        for step in (1, 2, 3):
+            origin = lax.rem(line + 4 - step, 4)
+            lanes = pl.ds(pl.multiple_of(origin * 128, 128), 128)
+            remote(
+                source.at[pl.ds(0, count)],
+                target.at[:, lanes],
+                act_send.at[row, step - 1],
+                act_recv.at[row, step - 1],
+                line_peer(at, step),
+            ).wait_recv()
+
+    mine = pl.ds(pl.multiple_of(core * HALF, 16), HALF)
+    own_copies = []
+
+    def step_line(index):
+        part = PARTS[index]
+        kind, unit = part
+        landing = pair_s if kind == "s" else pair_t
+        started[index].wait_recv()
+        if kind == "s":
+            low = ws_in[unit, mine].astype(F32)
+            high = landing[unit].astype(F32)
+            first = jnp.where(core == 0, low, high)
+            second = jnp.where(core == 0, high, low)
+            stage_s[unit, 0] = jnp.concatenate([first, second], axis=1).astype(BF16)
+            staged = stage_s.at[unit]
+        else:
+            low = wt_in[unit, mine].astype(F32)
+            high = landing[unit].astype(F32)
+            first = jnp.where(core == 0, low, high)
+            second = jnp.where(core == 0, high, low)
+            for tau in range(3):
+                lanes = slice(64 * tau, 64 * tau + 64)
+                stage_t[unit, tau, 0] = jnp.concatenate(
+                    [first[:, lanes], second[:, lanes]], axis=1
+                ).astype(BF16)
+            staged = stage_t.at[unit]
+        target = area(part, core, chip, line, 1)
+        for step in (1, 2, 3):
+            send(
+                remote(
+                    staged,
+                    target,
+                    line_send.at[index, step - 1],
+                    line_recv.at[index, step - 1],
+                    line_peer(at, step),
+                )
+            )
+        own = pltpu.make_async_copy(staged, target, own_sem.at[4 + index])
+        own.start()
+        own_copies.append(own)
+
+    def step_plane(index):
+        part = PARTS[index]
+        for step in (1, 2, 3):
+            origin = area(part, core, chip, lax.rem(line + 4 - step, 4), 1)
+            remote(
+                origin,
+                origin,
+                line_send.at[index, step - 1],
+                line_recv.at[index, step - 1],
+                line_peer(at, step),
+            ).wait_recv()
+        own_copies[index].wait()
+        held = area(part, core, chip, 0, 4)
+        for way, name in enumerate(("x", "y")):
+            send(
+                remote(held, held, plane_send.at[index, way], plane_recv.at[index, way], at[name])
+            )
+        send(remote(held, held, core_send.at[index, 0], core_recv.at[index, 0], at["pair"]))
+
+    def step_diag(index):
+        part = PARTS[index]
+        for way, (name, other, first) in enumerate((("x", "y", 0), ("y", "x", 2))):
+            held = area(part, core, at["chip_" + name], 0, 4)
+            remote(
+                held, held, plane_send.at[index, way], plane_recv.at[index, way], at[name]
+            ).wait_recv()
+            half = area(part, core, at["chip_" + name], first, 2)
+            send(
+                remote(half, half, diag_send.at[index, way], diag_recv.at[index, way], at[other])
+            )
+            send(
+                remote(
+                    held, held, core_send.at[index, 1 + way], core_recv.at[index, 1 + way], at["pair"]
+                )
+            )
+
+    def step_core(index):
+        part = PARTS[index]
+        for way, (other, first) in enumerate((("y", 0), ("x", 2))):
+            half = area(part, core, at["chip_d"], first, 2)
+            remote(
+                half, half, diag_send.at[index, way], diag_recv.at[index, way], at[other]
+            ).wait_recv()
+        held = area(part, core, at["chip_d"], 0, 4)
+        send(remote(held, held, core_send.at[index, 3], core_recv.at[index, 3], at["pair"]))
+
+    def step_end(index):
+        part = PARTS[index]
+        for slot, name in enumerate(("chip", "chip_x", "chip_y", "chip_d")):
+            held = area(part, 1 - core, at[name], 0, 4)
+            remote(
+                held, held, core_send.at[index, slot], core_recv.at[index, slot], at["pair"]
+            ).wait_recv()
+
+    step_line(0)
+    feat_own = acts(0, feat_in, feat_out, ROWS)
+    step_line(1)
+    for step in (1, 2, 3):
+        send(
+            remote(
+                par_in,
+                par_out.at[line],
+                act_send.at[2, step - 1],
+                act_recv.at[2, step - 1],
+                line_peer(at, step),
+            )
+        )
+    par_own = pltpu.make_async_copy(par_in, par_out.at[line], own_sem.at[2])
+    par_own.start()
+    step_line(2)
+    cot_own = acts(1, cot_in, cot_out, ROWS)
+    step_line(3)
+    step_plane(0)
+    step_plane(1)
+    step_diag(0)
+    step_plane(2)
+    step_diag(1)
+    step_core(0)
+    step_end(0)
+    step_plane(3)
+    step_diag(2)
+    step_core(1)
+    step_end(1)
+    step_diag(3)
+    step_core(2)
+    step_end(2)
+    step_core(3)
+    step_end(3)
+    acts_wait(0, feat_in, feat_out, ROWS)
+    acts_wait(1, cot_in, cot_out, ROWS)
+    for step in (1, 2, 3):
+        remote(
+            par_in,
+            par_out.at[lax.rem(line + 4 - step, 4)],
+            act_send.at[2, step - 1],
+            act_recv.at[2, step - 1],
+            line_peer(at, step),
+        ).wait_recv()
+    for own in (feat_own, cot_own, par_own):
+        own.wait()
+    for copy in started:
+        copy.wait_send()
+
+
+def rows_of(pixel):
+    return pl.ds(pl.multiple_of(pixel * SLOTS, SLOTS), SLOTS)
+
+
+def slope_of(values):
+    sigmoid = jax.nn.sigmoid(values)
+    return sigmoid * (1.0 + values * (1.0 - sigmoid))
+
+
+def block_kernel(
+    ws,
+    wt,
+    feat_in,
+    cot_in,
+    shuffle,
+    mask_in,
+    mid_in,
+    out_in,
+    block_out,
+    input_out,
+    grad_s,
+    grad_t,
+    mid_grad,
+    out_grad,
+    a_pad,
+    s_ref,
+    u_ref,
+    t_ref,
+    side,
+    feat_ref,
+    skip_ref,
+    wide,
+    ds_pad,
+    thin,
+    d_ref,
+    w_buf,
+    wt_buf,
+    g_buf,
+    land_mid,
+    land_mid_two,
+    land_out,
+    land_out_two,
+    w_sem,
+    wt_sem,
+    g_sem,
+    one_send,
+    one_recv,
+    two_send,
+    two_recv,
+):
+    at = place()
+    dp, line = at["dp"], at["line"]
+
+    def ring_peer(step):
+        return (lax.rem(dp + step, 8), line)
+
+    greet([ring_peer(step) for step in range(1, 8)] + [line_peer(at, step) for step in (1, 2, 3)])
+
+    mask_mid = mask_in[...]
+    mask_out = mask_in[:, :BLOCK_C]
+    slot_rows = lax.broadcasted_iota(jnp.int32, (SLOTS, BLOCK_C), 0)
+    has_before = (slot_rows >= 4).astype(F32)
+    has_after = (slot_rows < 12).astype(F32)
+
+    def fetch_w(unit, tap, slot):
+        lanes = pl.ds(pl.multiple_of(tap * BLOCK_C, 128), BLOCK_C)
+        return pltpu.make_async_copy(ws.at[unit, :, lanes], w_buf.at[slot], w_sem.at[slot])
+
+    def fetch_wt(unit):
+        return pltpu.make_async_copy(wt.at[unit], wt_buf, wt_sem.at[0])
+
+    def over_taps(unit, use):
+        fetch_w(unit, 0, 0).start()
+
+        def body(tap, carry):
+            slot = lax.rem(tap, 2)
+
+            @pl.when(tap < 8)
+            def _():
+                fetch_w(unit, tap + 1, 1 - slot).start()
+
+            fetch_w(unit, tap, slot).wait()
+            use(tap, slot)
+            return carry
+
+        lax.fori_loop(0, 9, body, 0)
+
+    def over_pixels(body, carry):
+        return lax.fori_loop(0, HW, body, carry)
+
+    def exchange(land, land_two, index, sem_index, count, payload, combine):
+        for row, value in enumerate(payload):
+            land[index, dp, row : row + 1, :] = value
+        sent = []
+        for step in range(1, 8):
+            here = land.at[index, dp, pl.ds(0, count)]
+            copy = remote(
+                here,
+                here,
+                one_send.at[sem_index, step - 1],
+                one_recv.at[sem_index, step - 1],
+                ring_peer(step),
+            )
+            copy.start()
+            sent.append(copy)
+        for step in range(1, 8):
+            there = land.at[index, lax.rem(dp + 8 - step, 8), pl.ds(0, count)]
+            remote(
+                there,
+                there,
+                one_send.at[sem_index, step - 1],
+                one_recv.at[sem_index, step - 1],
+                ring_peer(step),
+            ).wait_recv()
+        for copy in sent:
+            copy.wait_send()
+        merged = combine([land[index, source] for source in range(8)])
+        for row, value in enumerate(merged):
+            land_two[index, line, row : row + 1, :] = value
+        sent = []
+        for step in (1, 2, 3):
+            here = land_two.at[index, line, pl.ds(0, count)]
+            copy = remote(
+                here,
+                here,
+                two_send.at[sem_index, step - 1],
+                two_recv.at[sem_index, step - 1],
+                line_peer(at, step),
+            )
+            copy.start()
+            sent.append(copy)
+        for step in (1, 2, 3):
+            there = land_two.at[index, lax.rem(line + 4 - step, 4), pl.ds(0, count)]
+            remote(
+                there,
+                there,
+                two_send.at[sem_index, step - 1],
+                two_recv.at[sem_index, step - 1],
+                line_peer(at, step),
+            ).wait_recv()
+        for copy in sent:
+            copy.wait_send()
+        return combine([land_two[index, source] for source in range(4)])
+
+    def combine_moments(blocks):
+        total = sum(block[2:3] for block in blocks)
+        mean = sum(block[2:3] * block[0:1] for block in blocks) / total
+        spread = sum(
+            block[1:2] + block[2:3] * (block[0:1] - mean) * (block[0:1] - mean) for block in blocks
+        )
+        return [mean, spread, total]
+
+    def combine_sums(blocks):
+        return [sum(block[0:1] for block in blocks), sum(block[1:2] for block in blocks)]
+
+    def moments(values, mask, land, land_two, index, sem_index):
+        width = mask.shape[1]
+        zero = jnp.zeros((SLOTS, width), F32)
+        local = HW * jnp.sum(mask, axis=0, keepdims=True)
+        added = over_pixels(lambda p, acc: acc + values[rows_of(p), :], zero)
+        mean = jnp.sum(added * mask, axis=0, keepdims=True) / local
+
+        def squares(p, acc):
+            centered = values[rows_of(p), :] - mean
+            return acc + centered * centered
+
+        spread = jnp.sum(over_pixels(squares, zero) * mask, axis=0, keepdims=True)
+        mean, spread, total = exchange(
+            land, land_two, index, sem_index, 4, [mean, spread, local, local], combine_moments_four
+        )
+        return mean, lax.rsqrt(spread / total + EPS_NORM), total
+
+    def combine_moments_four(blocks):
+        mean, spread, total = combine_moments(blocks)
+        return [mean, spread, total]
+
+    for unit in range(2):
+        a_pad[unit] = jnp.zeros(a_pad.shape[1:], BF16)
+    ds_pad[...] = jnp.zeros(ds_pad.shape, BF16)
+    fetch_wt(0).start()
+    permute = shuffle[...]
+    feat_ref[...] = lax.dot_general(permute, feat_in[...], NN, preferred_element_type=F32).astype(
+        BF16
+    )
+
+    def fill(p, carry):
+        a_pad[0, 1 + p // SIDE, 1 + p % SIDE] = feat_ref[rows_of(p), :]
+        return carry
+
+    over_pixels(fill, 0)
+
+    def window(unit, tap):
+        return a_pad[unit, pl.ds(tap // 3, SIDE), pl.ds(tap % 3, SIDE)].reshape(ROWS, BLOCK_C)
+
+    stats_mid = []
+    stats_out = []
+    for unit in range(2):
+        gain, bias = mid_in[2 * unit : 2 * unit + 1], mid_in[2 * unit + 1 : 2 * unit + 2]
+
+        def conv(tap, slot):
+            value = lax.dot_general(
+                window(unit, tap), w_buf[slot], NT, preferred_element_type=F32
+            )
+
+            @pl.when(tap == 0)
+            def _():
+                s_ref[unit] = value
+
+            @pl.when(tap > 0)
+            def _():
+                s_ref[unit] = s_ref[unit] + value
+
+        over_taps(unit, conv)
+        mean, inverse, total = moments(
+            s_ref.at[unit], mask_mid, land_mid, land_mid_two, unit, 2 * unit
+        )
+        stats_mid.append((inverse, total))
+
+        def mid_act(p, carry):
+            rows = rows_of(p)
+            standard = (s_ref[unit, rows, :] - mean) * inverse
+            s_ref[unit, rows, :] = standard
+            normed = standard * gain + bias
+            u_ref[unit, rows, :] = (jax.nn.sigmoid(normed) * normed * mask_mid).astype(BF16)
+            return carry
+
+        over_pixels(mid_act, 0)
+        fetch_wt(unit).wait()
+        t_ref[unit] = lax.dot_general(u_ref[unit], wt_buf[1], NN, preferred_element_type=F32)
+        side[0] = lax.dot_general(u_ref[unit], wt_buf[0], NN, preferred_element_type=F32)
+        side[1] = lax.dot_general(u_ref[unit], wt_buf[2], NN, preferred_element_type=F32)
+        if unit == 0:
+            fetch_wt(1).start()
+
+        def frames(p, carry):
+            rows = rows_of(p)
+            t_ref[unit, rows, :] = (
+                t_ref[unit, rows, :]
+                + pltpu.roll(side[0, rows, :], 4, 0) * has_before
+                + pltpu.roll(side[1, rows, :], 12, 0) * has_after
+            )
+            return carry
+
+        over_pixels(frames, 0)
+        mean, inverse, total = moments(
+            t_ref.at[unit], mask_out, land_out, land_out_two, unit, 2 * unit + 1
+        )
+        stats_out.append((inverse, total))
+        gain, bias = out_in[2 * unit : 2 * unit + 1], out_in[2 * unit + 1 : 2 * unit + 2]
+        if unit == 0:
+
+            def out_act(p, carry):
+                rows = rows_of(p)
+                standard = (t_ref[0, rows, :] - mean) * inverse
+                t_ref[0, rows, :] = standard
+                normed = standard * gain + bias
+                hidden = jax.nn.sigmoid(normed) * normed * mask_out
+                a_pad[1, 1 + p // SIDE, 1 + p % SIDE] = hidden.astype(BF16)
+                return carry
+
+            over_pixels(out_act, 0)
+        else:
+            side[0] = lax.dot_general(permute, cot_in[...], NN, preferred_element_type=F32)
+
+            def end_act(p, carry):
+                rows = rows_of(p)
+                standard = (t_ref[1, rows, :] - mean) * inverse
+                t_ref[1, rows, :] = standard
+                pre = standard * gain + bias + feat_ref[rows, :].astype(F32)
+                sigmoid = jax.nn.sigmoid(pre)
+                thin[rows, :] = (pre * sigmoid * mask_out).astype(BF16)
+                slope = sigmoid * (1.0 + pre * (1.0 - sigmoid))
+                skip = side[0, rows, :] * mask_out * slope
+                skip_ref[rows, :] = skip
+                side[1, rows, :] = skip
+                return carry
+
+            over_pixels(end_act, 0)
+            block_out[...] = lax.dot_general(
+                permute, thin[...], TN, preferred_element_type=F32
+            ).astype(BF16)
+
+    zero_mid = jnp.zeros((SLOTS, MID_C), F32)
+    zero_out = jnp.zeros((SLOTS, BLOCK_C), F32)
+
+    def put_grad(target, slot):
+        return pltpu.make_async_copy(g_buf.at[slot], target, g_sem.at[slot])
+
+    for unit in (1, 0):
+        gain = out_in[2 * unit : 2 * unit + 1]
+        inverse, total = stats_out[unit]
+
+        def out_sums(p, carry):
+            rows = rows_of(p)
+            grad = side[1, rows, :]
+            return (carry[0] + grad, carry[1] + grad * t_ref[unit, rows, :])
+
+        bias_acc, gain_acc = over_pixels(out_sums, (zero_out, zero_out))
+        sums = [
+            jnp.sum(bias_acc, axis=0, keepdims=True),
+            jnp.sum(gain_acc, axis=0, keepdims=True),
+        ]
+        grad_bias, grad_gain = exchange(
+            land_out, land_out_two, 2 + unit, 5 + 2 * unit, 2, sums, combine_sums
+        )
+        out_grad[2 * unit : 2 * unit + 1, :] = grad_gain
+        out_grad[2 * unit + 1 : 2 * unit + 2, :] = grad_bias
+        scale = gain * inverse
+        bias_part, gain_part = grad_bias / total, grad_gain / total
+
+        def out_back(p, carry):
+            rows = rows_of(p)
+            value = (
+                mask_out
+                * scale
+                * (side[1, rows, :] - bias_part - t_ref[unit, rows, :] * gain_part)
+            )
+            d_ref[1, rows, :] = value.astype(BF16)
+            d_ref[0, rows, :] = (pltpu.roll(value, 12, 0) * has_after).astype(BF16)
+            d_ref[2, rows, :] = (pltpu.roll(value, 4, 0) * has_before).astype(BF16)
+            return carry
+
+        over_pixels(out_back, 0)
+        if unit == 0:
+            fetch_wt(0).wait()
+
+        for tau in range(3):
+            slot = tau % 2
+            if tau == 2:
+                put_grad(grad_t.at[unit, 0], slot).wait()
+            g_buf[slot] = lax.dot_general(
+                u_ref[unit], d_ref[tau], TN, preferred_element_type=F32
+            ).astype(BF16)
+            put_grad(grad_t.at[unit, tau], slot).start()
+            value = lax.dot_general(d_ref[tau], wt_buf[tau], NT, preferred_element_type=F32)
+            wide[...] = value if tau == 0 else wide[...] + value
+        put_grad(grad_t.at[unit, 1], 1).wait()
+        put_grad(grad_t.at[unit, 2], 0).wait()
+        if unit == 1:
+            fetch_wt(0).start()
+
+        gain, bias = mid_in[2 * unit : 2 * unit + 1], mid_in[2 * unit + 1 : 2 * unit + 2]
+        inverse, total = stats_mid[unit]
+
+        def mid_sums(p, carry):
+            rows = rows_of(p)
+            standard = s_ref[unit, rows, :]
+            grad = mask_mid * slope_of(standard * gain + bias) * wide[rows, :]
+            wide[rows, :] = grad
+            return (carry[0] + grad, carry[1] + grad * standard)
+
+        bias_acc, gain_acc = over_pixels(mid_sums, (zero_mid, zero_mid))
+        sums = [
+            jnp.sum(bias_acc, axis=0, keepdims=True),
+            jnp.sum(gain_acc, axis=0, keepdims=True),
+        ]
+        grad_bias, grad_gain = exchange(
+            land_mid, land_mid_two, 2 + unit, 4 + 2 * unit, 2, sums, combine_sums
+        )
+        mid_grad[2 * unit : 2 * unit + 1, :] = grad_gain
+        mid_grad[2 * unit + 1 : 2 * unit + 2, :] = grad_bias
+        scale = gain * inverse
+        bias_part, gain_part = grad_bias / total, grad_gain / total
+
+        def mid_back(p, carry):
+            rows = rows_of(p)
+            value = (
+                mask_mid
+                * scale
+                * (wide[rows, :] - bias_part - s_ref[unit, rows, :] * gain_part)
+            )
+            ds_pad[1 + p // SIDE, 1 + p % SIDE] = value.astype(BF16)
+            return carry
+
+        over_pixels(mid_back, 0)
+
+        def grad_lanes(tap):
+            return grad_s.at[unit, :, pl.ds(pl.multiple_of(tap * BLOCK_C, 128), BLOCK_C)]
+
+        def back(tap, slot):
+            @pl.when(tap >= 2)
+            def _():
+                put_grad(grad_lanes(tap - 2), slot).wait()
+
+            inner = ds_pad[1 : 1 + SIDE, 1 : 1 + SIDE].reshape(ROWS, MID_C)
+            g_buf[slot] = lax.dot_general(
+                inner, window(unit, tap), TN, preferred_element_type=F32
+            ).astype(BF16)
+            put_grad(grad_lanes(tap), slot).start()
+            moved = ds_pad[pl.ds(2 - tap // 3, SIDE), pl.ds(2 - tap % 3, SIDE)].reshape(ROWS, MID_C)
+            value = lax.dot_general(moved, w_buf[slot], NN, preferred_element_type=F32)
+
+            @pl.when(tap == 0)
+            def _():
+                side[0] = value
+
+            @pl.when(tap > 0)
+            def _():
+                side[0] = side[0] + value
+
+        over_taps(unit, back)
+        put_grad(grad_lanes(7), 1).wait()
+        put_grad(grad_lanes(8), 0).wait()
+        if unit == 1:
+            gain, bias = out_in[0:1], out_in[1:2]
+
+            def hidden_back(p, carry):
+                rows = rows_of(p)
+                slope = slope_of(t_ref[0, rows, :] * gain + bias)
+                side[1, rows, :] = mask_out * slope * side[0, rows, :]
+                return carry
+
+            over_pixels(hidden_back, 0)
+
+    thin[...] = (side[0] + skip_ref[...]).astype(BF16)
+    input_out[...] = lax.dot_general(permute, thin[...], TN, preferred_element_type=F32).astype(
+        BF16
+    )
+
+
+def scatter_kernel(
+    grad_s,
+    grad_t,
+    block_in,
+    input_in,
+    sum_s,
+    sum_t,
+    block_out,
+    input_out,
+    own_s,
+    own_t,
+    land_s,
+    land_t,
+    one_s,
+    one_t,
+    two_s,
+    two_t,
+    part_s,
+    part_t,
+    line_s,
+    line_t,
+    fin_s,
+    fin_t,
+    act_send,
+    act_recv,
+    core_send,
+    core_recv,
+    one_send,
+    one_recv,
+    two_send,
+    two_recv,
+    line_send,
+    line_recv,
+    fin_send,
+    fin_recv,
+    own_sem,
+):
+    at = place()
+    line, core, chip = at["line"], at["core"], at["chip"]
+    greet([at["pair"], at["x"], at["y"]] + [line_peer(at, step) for step in (1, 2, 3)])
+    started = []
+
+    def send(copy):
+        copy.start()
+        started.append(copy)
+
+    def pick(part, small, large):
+        return large if part[0] == "s" else small
+
+    def grads(part, half):
+        if part[0] == "s":
+            return grad_s.at[part[1], :, half]
+        return grad_t.at[part[1], :, :, half]
+
+    def lanes_of(part, owner):
+        width = pick(part, CHIP_T, CHIP_S)
+        return pl.ds(pl.multiple_of(owner * width, 128), width)
+
+    def cut(part, owner, first, count):
+        ref = pick(part, own_t, own_s)
+        lanes = lanes_of(part, owner)
+        if part[0] == "s":
+            return ref.at[part[1], pl.ds(first, count), :, lanes]
+        return ref.at[part[1], :, pl.ds(first, count), :, lanes]
+
+    def some(ref, part, first, count):
+        if part[0] == "s":
+            return ref.at[part[1], pl.ds(first, count)]
+        return ref.at[part[1], :, pl.ds(first, count)]
+
+    own_copies = []
+    for index, part in enumerate(PARTS):
+        landing = pick(part, land_t, land_s).at[part[1]]
+        send(
+            remote(
+                grads(part, 1 - core),
+                landing,
+                core_send.at[index],
+                core_recv.at[index],
+                at["pair"],
+            )
+        )
+        own = pltpu.make_async_copy(
+            grads(part, core), pick(part, own_t, own_s).at[part[1]], own_sem.at[index]
+        )
+        own.start()
+        own_copies.append(own)
+    act_copies = []
+    lanes_line = pl.ds(pl.multiple_of(line * 128, 128), 128)
+    rows_line = pl.ds(pl.multiple_of(line * ROWS, 16), ROWS)
+    for row, (source, target) in enumerate(((block_in, block_out), (input_in, input_out))):
+        for step in (1, 2, 3):
+            peer = line_peer(at, step)
+            send(
+                remote(
+                    source.at[:, pl.ds(pl.multiple_of(peer[1] * 128, 128), 128)],
+                    target.at[rows_line],
+                    act_send.at[row, step - 1],
+                    act_recv.at[row, step - 1],
+                    peer,
+                )
+            )
+        own = pltpu.make_async_copy(
+            source.at[:, lanes_line], target.at[rows_line], own_sem.at[4 + row]
+        )
+        own.start()
+        act_copies.append(own)
+
+    def add_into(target, source, shape):
+        outer = int(np.prod(shape[:-2]))
+        step = 16 if shape[-1] > 2048 else HALF
+        per = HALF // step
+
+        def body(index, carry):
+            place_in = lax.div(index, per)
+            rows = pl.ds(pl.multiple_of(lax.rem(index, per) * step, 16), step)
+            if len(shape) == 3:
+                where = (place_in, rows)
+            else:
+                where = (lax.div(place_in, shape[1]), lax.rem(place_in, shape[1]), rows)
+            target[where] = (target[where].astype(F32) + source[where].astype(F32)).astype(BF16)
+            return carry
+
+        lax.fori_loop(0, outer * per, body, 0)
+
+    def step_one(index):
+        part = PARTS[index]
+        own_copies[index].wait()
+        started[index].wait_recv()
+        own, land = pick(part, own_t, own_s).at[part[1]], pick(part, land_t, land_s).at[part[1]]
+        add_into(own, land, own.shape)
+        ones, twos = pick(part, one_t, one_s), pick(part, two_t, two_s)
+        for way, (name, first) in enumerate((("x", 0), ("y", 2))):
+            send(
+                remote(
+                    cut(part, at["chip_d"], first, 2),
+                    ones.at[part[1], way],
+                    one_send.at[index, way],
+                    one_recv.at[index, way],
+                    at[name],
+                )
+            )
+            send(
+                remote(
+                    cut(part, at["chip_" + name], first, 2),
+                    some(twos.at[:, way], part, first, 2),
+                    two_send.at[index, way, 0],
+                    two_recv.at[index, way, 0],
+                    at[name],
+                )
+            )
+
+    def step_two(index):
+        part = PARTS[index]
+        ones, twos = pick(part, one_t, one_s), pick(part, two_t, two_s)
+        for way, (name, other, first) in enumerate((("x", "y", 0), ("y", "x", 2))):
+            landing = ones.at[part[1], way]
+            remote(
+                landing,
+                landing,
+                one_send.at[index, way],
+                one_recv.at[index, way],
+                at[name],
+            ).wait_recv()
+            target = cut(part, at["chip_" + other], first, 2)
+            add_into(target, landing, target.shape)
+            send(
+                remote(
+                    target,
+                    some(twos.at[:, 1 - way], part, first, 2),
+                    two_send.at[index, 1 - way, 1],
+                    two_recv.at[index, 1 - way, 1],
+                    at[other],
+                )
+            )
+
+    def step_three(index):
+        part = PARTS[index]
+        unit = part[1]
+        twos = pick(part, two_t, two_s)
+        for way, (name, first) in enumerate((("x", 0), ("y", 2))):
+            for turn, begin in enumerate((first, 2 - first)):
+                landing = some(twos.at[:, way], part, begin, 2)
+                remote(
+                    landing,
+                    landing,
+                    two_send.at[index, way, turn],
+                    two_recv.at[index, way, turn],
+                    at[name],
+                ).wait_recv()
+        own = cut(part, chip, 0, 4)
+        target = pick(part, part_t, part_s)
+
+        def body(owner, carry):
+            if part[0] == "s":
+                target[unit, owner] = (
+                    own[owner].astype(F32)
+                    + twos[unit, 0, owner].astype(F32)
+                    + twos[unit, 1, owner].astype(F32)
+                ).astype(BF16)
+            else:
+                for tau in range(3):
+                    target[unit, owner, tau] = (
+                        own[tau, owner].astype(F32)
+                        + twos[unit, 0, tau, owner].astype(F32)
+                        + twos[unit, 1, tau, owner].astype(F32)
+                    ).astype(BF16)
+            return carry
+
+        lax.fori_loop(0, 4, body, 0)
+        lines = pick(part, line_t, line_s)
+        for step in (1, 2, 3):
+            peer = line_peer(at, step)
+            send(
+                remote(
+                    target.at[unit, peer[1]],
+                    lines.at[unit, step - 1],
+                    line_send.at[index, step - 1],
+                    line_recv.at[index, step - 1],
+                    peer,
+                )
+            )
+
+    fin_copies = [None] * 4
+
+    def step_four(index):
+        part = PARTS[index]
+        unit = part[1]
+        lines, target, fin = (
+            pick(part, line_t, line_s),
+            pick(part, part_t, part_s),
+            pick(part, fin_t, fin_s),
+        )
+        for step in (1, 2, 3):
+            landing = lines.at[unit, step - 1]
+            remote(
+                landing,
+                landing,
+                line_send.at[index, step - 1],
+                line_recv.at[index, step - 1],
+                line_peer(at, step),
+            ).wait_recv()
+        total = target[unit, line].astype(F32)
+        for step in range(3):
+            total = total + lines[unit, step].astype(F32)
+        fin[unit, 0] = total
+        copy = remote(
+            fin.at[unit, 0], fin.at[unit, 1], fin_send.at[index], fin_recv.at[index], at["pair"]
+        )
+        send(copy)
+        fin_copies[index] = copy
+
+    def step_five(index):
+        part = PARTS[index]
+        unit = part[1]
+        fin_copies[index].wait_recv()
+        fin = pick(part, fin_t, fin_s)
+        for which in range(2):
+            half = core if which == 0 else 1 - core
+            rows = pl.ds(pl.multiple_of(half * HALF, 16), HALF)
+            if part[0] == "s":
+                value = fin[unit, which]
+                width = CHIP_S // 2
+                sum_s[unit, rows, :] = jnp.where(core == 0, value[:, :width], value[:, width:])
+            else:
+                width = CHIP_T // 2
+                for tau in range(3):
+                    value = fin[unit, which, tau]
+                    sum_t[unit, tau, rows, :] = jnp.where(
+                        core == 0, value[:, :width], value[:, width:]
+                    )
+
+    order = (2, 3, 1, 0)
+    step_one(order[0])
+    step_one(order[1])
+    step_two(order[0])
+    step_one(order[2])
+    step_two(order[1])
+    step_one(order[3])
+    step_three(order[0])
+    step_two(order[2])
+    step_three(order[1])
+    step_two(order[3])
+    step_four(order[0])
+    step_three(order[2])
+    step_four(order[1])
+    step_three(order[3])
+    step_five(order[0])
+    step_five(order[1])
+    step_four(order[2])
+    step_five(order[2])
+    step_four(order[3])
+    step_five(order[3])
+    for row, (source, target) in enumerate(((block_in, block_out), (input_in, input_out))):
+        for step in (1, 2, 3):
+            origin = lax.rem(line + 4 - step, 4)
+            remote(
+                source.at[:, lanes_line],
+                target.at[pl.ds(pl.multiple_of(origin * ROWS, 16), ROWS)],
+                act_send.at[row, step - 1],
+                act_recv.at[row, step - 1],
+                line_peer(at, step),
+            ).wait_recv()
+        act_copies[row].wait()
+    for copy in started:
+        copy.wait_send()
+
+
+def spaces(text):
+    return [pl.BlockSpec(memory_space=VMEM if mark == "v" else pl.ANY) for mark in text]
+
+
+def dma(*shape):
+    return pltpu.SemaphoreType.DMA(shape)
+
+
+def params(number):
+    return pltpu.CompilerParams(
+        collective_id=number, has_side_effects=True, vmem_limit_bytes=GRANT
+    )
+
+
+def gather_all(ws, wt, feat, cot, par):
+    return pl.pallas_call(
+        gather_kernel,
+        out_shape=[
+            jax.ShapeDtypeStruct((2, 4, 2, HALF, TAPS_C), BF16),
+            jax.ShapeDtypeStruct((2, 3, 4, 2, HALF, BLOCK_C), BF16),
+            jax.ShapeDtypeStruct((ROWS, BLOCK_C), BF16),
+            jax.ShapeDtypeStruct((ROWS, BLOCK_C), BF16),
+            jax.ShapeDtypeStruct((4,) + par.shape, F32),
+        ],
+        in_specs=spaces("vvaav"),
+        out_specs=spaces("aaaaa"),
+        scratch_shapes=[
+            VMEM((2, HALF, CHIP_S // 2), BF16),
+            VMEM((2, HALF, 3 * CHIP_T // 2), BF16),
+            VMEM((2, 1, HALF, CHIP_S), BF16),
+            VMEM((2, 3, 1, HALF, CHIP_T), BF16),
+            dma(4),
+            dma(4),
+            dma(3, 3),
+            dma(3, 3),
+            dma(4, 3),
+            dma(4, 3),
+            dma(4, 2),
+            dma(4, 2),
+            dma(4, 2),
+            dma(4, 2),
+            dma(4, 4),
+            dma(4, 4),
+            dma(8),
+        ],
+        compiler_params=params(0),
+        name="gather_all",
+    )(ws, wt, feat, cot, par)
+
+
+def run_block(ws, wt, feat, cot, shuffle, mask, mid, out):
+    return pl.pallas_call(
+        block_kernel,
+        out_shape=[
+            jax.ShapeDtypeStruct((ROWS, BLOCK_C), BF16),
+            jax.ShapeDtypeStruct((ROWS, BLOCK_C), BF16),
+            jax.ShapeDtypeStruct((2, MID_C, TAPS_C), BF16),
+            jax.ShapeDtypeStruct((2, 3, MID_C, BLOCK_C), BF16),
+            jax.ShapeDtypeStruct((4, MID_C), F32),
+            jax.ShapeDtypeStruct((4, BLOCK_C), F32),
+        ],
+        in_specs=spaces("aavvvvvv"),
+        out_specs=spaces("vvaavv"),
+        scratch_shapes=[
+            VMEM((2, SIDE + 2, SIDE + 2, SLOTS, BLOCK_C), BF16),
+            VMEM((2, ROWS, MID_C), F32),
+            VMEM((2, ROWS, MID_C), BF16),
+            VMEM((2, ROWS, BLOCK_C), F32),
+            VMEM((2, ROWS, BLOCK_C), F32),
+            VMEM((ROWS, BLOCK_C), BF16),
+            VMEM((ROWS, BLOCK_C), F32),
+            VMEM((ROWS, MID_C), F32),
+            VMEM((SIDE + 2, SIDE + 2, SLOTS, MID_C), BF16),
+            VMEM((ROWS, BLOCK_C), BF16),
+            VMEM((3, ROWS, BLOCK_C), BF16),
+            VMEM((2, MID_C, BLOCK_C), BF16),
+            VMEM((3, MID_C, BLOCK_C), BF16),
+            VMEM((2, MID_C, BLOCK_C), BF16),
+            VMEM((4, 8, 8, MID_C), F32),
+            VMEM((4, 4, 8, MID_C), F32),
+            VMEM((4, 8, 8, BLOCK_C), F32),
+            VMEM((4, 4, 8, BLOCK_C), F32),
+            dma(2),
+            dma(1),
+            dma(2),
+            dma(8, 7),
+            dma(8, 7),
+            dma(8, 3),
+            dma(8, 3),
+        ],
+        compiler_params=params(1),
+        name="run_block",
+    )(ws, wt, feat, cot, shuffle, mask, mid, out)
+
+
+def scatter_all(grad_s, grad_t, block, grad_in):
+    return pl.pallas_call(
+        scatter_kernel,
+        out_shape=[
+            jax.ShapeDtypeStruct((2, 2 * HALF, CHIP_S // 2), F32),
+            jax.ShapeDtypeStruct((2, 3, 2 * HALF, CHIP_T // 2), F32),
+            jax.ShapeDtypeStruct((4 * ROWS, 128), BF16),
+            jax.ShapeDtypeStruct((4 * ROWS, 128), BF16),
+        ],
+        in_specs=spaces("aavv"),
+        out_specs=spaces("vvaa"),
+        scratch_shapes=[
+            VMEM((2, 4, HALF, TAPS_C), BF16),
+            VMEM((2, 3, 4, HALF, BLOCK_C), BF16),
+            VMEM((2, 4, HALF, TAPS_C), BF16),
+            VMEM((2, 3, 4, HALF, BLOCK_C), BF16),
+            VMEM((2, 2, 2, HALF, CHIP_S), BF16),
+            VMEM((2, 2, 3, 2, HALF, CHIP_T), BF16),
+            VMEM((2, 2, 4, HALF, CHIP_S), BF16),
+            VMEM((2, 2, 3, 4, HALF, CHIP_T), BF16),
+            VMEM((2, 4, HALF, CHIP_S), BF16),
+            VMEM((2, 4, 3, HALF, CHIP_T), BF16),
+            VMEM((2, 3, HALF, CHIP_S), BF16),
+            VMEM((2, 3, 3, HALF, CHIP_T), BF16),
+            VMEM((2, 2, HALF, CHIP_S), F32),
+            VMEM((2, 2, 3, HALF, CHIP_T), F32),
+            dma(2, 3),
+            dma(2, 3),
+            dma(4),
+            dma(4),
+            dma(4, 2),
+            dma(4, 2),
+            dma(4, 2, 2),
+            dma(4, 2, 2),
+            dma(4, 3),
+            dma(4, 3),
+            dma(4),
+            dma(4),
+            dma(8),
+        ],
+        compiler_params=params(2),
+        name="scatter_all",
+    )(grad_s, grad_t, block, grad_in)
+
+
+def shuffle_matrix():
+    clip, frame, pixel = np.meshgrid(np.arange(4), np.arange(FRAMES), np.arange(HW), indexing="ij")
+    source = (clip * FRAMES + frame) * HW + pixel
+    target = pixel * SLOTS + frame * 4 + clip
+    matrix = np.zeros((ROWS, ROWS), np.float32)
+    matrix[target.reshape(-1), source.reshape(-1)] = 1.0
+    return jnp.asarray(matrix, BF16)
+
+
+def on_pairs(
+    features,
+    cotangent,
+    clip_frames,
+    spatial_master,
+    spatial_first,
+    spatial_second,
+    temporal_master,
+    temporal_first,
+    temporal_second,
+    mid_norm,
+    mid_first,
+    mid_second,
+    out_norm,
+    out_first,
+    out_second,
+):
+    line = lax.axis_index("chan")
+    ws_own = jnp.swapaxes(spatial_master, 1, 2).astype(BF16)
+    wt_own = (
+        jnp.swapaxes(temporal_master, 1, 2).reshape(2, 2 * HALF, 3 * CHIP_T // 2).astype(BF16)
+    )
+    norm_pack = jnp.pad(
+        jnp.concatenate([mid_norm, out_norm], axis=1), ((0, 4), (0, 96))
+    )
+    ws, wt, feat, cot, norm_all = gather_all(
+        ws_own, wt_own, features, cotangent.astype(BF16), norm_pack
+    )
+    width = mid_norm.shape[1]
+    mid = jnp.swapaxes(norm_all[:, :4, :width], 0, 1).reshape(4, MID_C)
+    out = jnp.swapaxes(norm_all[:, :4, width : width + 128], 0, 1).reshape(4, BLOCK_C)
+    kept = clip_frames // 8
+    kept_own = lax.dynamic_slice_in_dim(kept, line * 4, 4)
+    frame_ids = jnp.arange(FRAMES, dtype=jnp.int32)
+    mask = (frame_ids[:, None] < kept_own[None, :]).astype(F32).reshape(SLOTS, 1)
+    mask = jnp.broadcast_to(mask, (SLOTS, MID_C))
+    block, grad_in, grad_s, grad_t, mid_all, out_all = run_block(
+        ws.reshape(2, MID_C, TAPS_C),
+        wt.reshape(2, 3, MID_C, BLOCK_C),
+        feat,
+        cot,
+        shuffle_matrix(),
+        mask,
+        mid,
+        out,
+    )
+    sum_s, sum_t, block_rows, grad_rows = scatter_all(
+        grad_s.reshape(2, 4, 2, HALF, TAPS_C),
+        grad_t.reshape(2, 3, 4, 2, HALF, BLOCK_C),
+        block,
+        grad_in,
+    )
+    block_out = block_rows.astype(F32)
+    clip_pool = (
+        jnp.sum(block_out.reshape(-1, FRAMES * HW, block_out.shape[1]), axis=1)
+        / (HW * kept.astype(F32))[:, None]
+    )
+    mid_grad = lax.dynamic_slice_in_dim(mid_all, line * width, width, axis=1)
+    out_grad = lax.dynamic_slice_in_dim(out_all, line * 128, 128, axis=1)
+    spatial = adam_update(
+        spatial_master,
+        spatial_first,
+        spatial_second,
+        jnp.swapaxes(sum_s, 1, 2),
+        RATE_CONV,
+        DECAY_CONV,
+    )
+    temporal = adam_update(
+        temporal_master, temporal_first, temporal_second, sum_t, RATE_CONV, DECAY_CONV
+    )
+    mid_new = adam_update(mid_norm, mid_first, mid_second, mid_grad, RATE_NORM, 0.0)
+    out_new = adam_update(out_norm, out_first, out_second, out_grad, RATE_NORM, 0.0)
+    return (
+        (block_out, clip_pool, grad_rows.astype(F32)) + spatial + temporal + mid_new + out_new
+    )
+
+
 def solution(mesh):
     in_specs = (
         P("dp", "chan"),
@@ -328,6 +1585,7 @@
         P(None, "chan"),
         P(None, "chan"),
     )
+    body = on_pairs if mesh.shape["dp"] == 8 and mesh.shape["chan"] == 4 else on_device
     return jax.shard_map(
-        on_device, mesh=mesh, in_specs=in_specs, out_specs=out_specs, check_vma=False
-    )
+        body, mesh=mesh, in_specs=in_specs, out_specs=out_specs, check_vma=False
+    )

time: 1460 us -> 588 us (0.40)
  Pallas kernels: 0 us -> 544 us
  waiting for transfers between devices: 533 us -> 0 us
  local copies, waits for them, and re-layouts: 411 us -> 17 us
  matrix products: 232 us -> 0 us
  blocking collectives: 157 us -> 0 us
  other arithmetic: 92.8 us -> 19.6 us
  between operations: 16.6 us -> 0.77 us
    pallas_call x0 -> x3, Pallas kernels: none -> 544 us  [the longest x1 200 us: run_block(): pl.pallas_call(block_kernel, out_shape=[jax.ShapeDtypeStruct((ROWS, BLOCK...]
    all_gather x6 -> x0, waiting for transfers between devices: 222 us -> none  [the longest x2 106 us: on_device(): lax.all_gather(grad_temporal.astype(jnp.bfloat16), 'chan', axis=1, tiled=...]
    unnamed x17 -> x0, waiting for transfers between devices: 211 us -> none
    psum x12 -> x0, blocking collectives: 157 us -> none  [the longest x4 55.3 us: normalize(): lax.psum((local_valid, jnp.sum(values * validity, axis=0)), 'dp')]
    reshape x27 -> x3, local copies, waits for them, and re-layouts: 147 us -> 3.45 us  [the longest x1 1.43 us: on_pairs(): jnp.swapaxes(norm_all[:, :4, width:width + 128], 0, 1).reshape(4, BLOCK_C)]
    dot_general x56 -> x0, matrix products: 125 us -> none  [the longest x18 35.6 us: spatial_grads(): lax.dot_general(window, grad_out, (((0,), (0,)), ((), ())), preferred_ele...]
    unnamed x339 -> x30, local copies, waits for them, and re-layouts: 122 us -> 11 us
    slice x16 -> x0, matrix products: 106 us -> none  [spatial_grads(): pulled[:, 2 - row_off:2 - row_off + SIDE, 2 - col_off:2 - col_off + SIDE]]
  transfers between devices with their start and end apart: 12 -> 0, of which waited for: 10 -> 0; matrix products, arithmetic and copies ran while one was open for 17% -> 0% of each run, Pallas kernels for 0% -> 0%
where the time goes in v1:
time: 588 us; the launch traced here: 582 us
  Pallas kernels  544 us (93%)
  other arithmetic  19.6 us (3%)
  local copies, waits for them, and re-layouts  17 us (3%)
    pallas_call x1, Pallas kernels, run_block(): pl.pallas_call(block_kernel, out_shape=[jax.ShapeDtypeStruct((ROWS, BLOCK...  200 us
    pallas_call x1, Pallas kernels, gather_all(): pl.pallas_call(gather_kernel, out_shape=[jax.ShapeDtypeStruct((2, 4, 2, H...  176 us
    pallas_call x1, Pallas kernels, scatter_all(): pl.pallas_call(scatter_kernel, out_shape=[jax.ShapeDtypeStruct((2, 2 * HA...  168 us

profile of v1, /device:TPU:0, one launch (start us, length us, event | category | flops | bytes accessed | tf_op | source)
XLA Modules:
  0.0 581.8 jit_solution(3890516593794840576)
XLA Ops:
  0.6 0.0 copy-start
  0.7 0.8 convert_multiply_fusion
  1.4 0.1 dynamic_slice.9
  1.5 0.1 reshape.80
  1.6 0.7 broadcast_in_dim.2.mask_in
  2.3 2.4 convert_element_type.41.cot_in
  4.7 0.0 copy-done
  4.7 0.0 copy-start.2
  4.7 0.0 copy-start.6
  4.7 0.0 copy-start.7
  4.7 0.9 convert_bitcast_fusion.ws_in
  5.7 0.3 copy-done.2
  6.0 0.9 copy.40.wt_in
  6.9 0.0 copy-done.6
  6.9 0.0 copy-done.7
  6.9 0.7 select_maximum_fusion.par_in
  7.6 176.4 %gather_all.1 = (bf16[2,4,2,144,4608]{4,3,2,1,0:T(8,128)(2,1)}, bf16[2,3,4,2,144,512]{5,4,3,2,1,0:T(8,128)(2,1)}, bf16[784,512]{1,0:T(8,128)(2,1)}, bf16[784,512]{1,0:T(8,128)(2,1)}, f32[4,8,512]{2,1,0:T(8,128)}) custom-call(bf16[2,288,576]{2,1,0:T(8,128)(2,1)} %convert_bitcast_fusion.ws_in, bf16[2,288,192]{2,1,0:T(8,128)(2,1)} %copy.40.wt_in, ...), custom_call_target="tpu_custom_call" | custom-call | tf_op jit(solution)/shard_map/gather_all/pallas_call | solution.py:1342
  184.0 0.8 slice_bitcast_fusion
  184.8 0.7 reshape.75.mid_in
  185.5 1.4 slice_bitcast_fusion.1.out_in
  186.9 200.3 %run_block.1 = (bf16[784,512]{1,0:T(8,128)(2,1)}, bf16[784,512]{1,0:T(8,128)(2,1)}, bf16[2,1152,4608]{2,1,0:T(8,128)(2,1)}, bf16[2,3,1152,512]{3,2,1,0:T(8,128)(...) custom-call(bf16[2,1152,4608]{2,1,0:T(8,128)(2,1)} %bitcast.22, bf16[2,3,1152,512]{3,2,1,0:T(8,128)(2,1)} %bitcast.24, ...), custom_call_target="tpu_custom_call" | custom-call | tf_op jit(solution)/shard_map/run_block/pallas_call | solution.py:1378
  387.3 167.6 %scatter_all.1 = (f32[2,288,576]{2,1,0:T(8,128)}, f32[2,3,288,64]{3,2,1,0:T(8,128)}, bf16[3136,128]{1,0:T(8,128)(2,1)}, bf16[3136,128]{1,0:T(8,128)(2,1)}) custom-call(bf16[2,4,2,144,4608]{4,3,2,1,0:T(8,128)(2,1)} %bitcast.23, bf16[2,3,4,2,144,512]{5,4,3,2,1,0:T(8,128)(2,1)} %bitcast.25, bf16[784,512]{1,0:T(8,128)(2,1)} %get-tuple-element.37.block_in, ...), custom_call_target="tpu_custom_call" | custom-call | tf_op jit(solution)/shard_map/scatter_all/pallas_call | solution.py:1423
  554.9 0.0 copy-start.5
  554.9 0.0 copy-start.3
  554.9 2.4 copy.42
  557.3 0.0 copy-done.5
  557.3 1.2 copy.43
  558.5 0.0 copy-done.3
  558.5 1.2 copy.45
  559.7 3.8 multiply_subtract_fusion.1
  563.6 2.3 copy.46
  565.9 2.3 copy.47
  568.2 1.2 copy.48
  569.4 5.0 multiply_subtract_fusion
  574.4 0.0 copy-start.1
  574.4 1.3 reshape.79
  575.8 0.1 reduce_sum.9
  575.9 0.0 copy-start.4
  575.9 0.7 broadcast_divide_fusion
  576.5 0.0 copy-done.1
  576.6 1.3 convert_element_type.44
  577.8 0.0 copy-start.8
  577.8 0.0 copy-start.9
  577.8 0.0 copy-start.10
  577.8 0.0 copy-start.11
  577.8 0.0 copy-done.4
  577.8 1.3 convert_element_type.46
  579.1 0.0 copy-done.8
  579.1 0.0 copy-done.9
  579.1 1.4 multiply_subtract_fusion.2
  580.5 0.0 copy-done.10
  580.5 0.0 copy-done.11
  580.5 1.3 multiply_subtract_fusion.3
  (3 shorter events, 0.1 us)
Async XLA Ops:
  0.6 4.1 copy-start
  4.7 1.2 copy-start.2
  4.7 2.2 copy-start.6
  4.7 2.2 copy-start.7
  554.9 2.4 copy-start.5
  554.9 3.6 copy-start.3
  574.4 2.1 copy-start.1
  575.9 2.0 copy-start.4
  577.8 1.3 copy-start.8
  577.8 1.3 copy-start.9
  577.8 2.7 copy-start.10
  577.8 2.7 copy-start.11
